TPU v7x, 32 devices: a whole 2x2x4 slice. The times are simulated.
32 devices in a mesh: lon: 4 (over y, x), lat: 8 (over z, core).
Axes of the slice: x: 2, y: 2, z: 4, core: 2. Of those that a mesh axis runs over, the one named last changes fastest.
Arguments:
- sensitivity: float32 [32, 1440, 128], P('lat', 'lon'), may hold values from -6 to 6
- courant_east: float32 [32, 1440, 32], P('lat', 'lon'), may hold values from -0.9 to 0.9
- courant_north: float32 [32, 1440, 32], P('lat', 'lon'), may hold values from -0.9 to 0.9
- mixing: float32 [32, 1440, 31], P('lat', 'lon'), may hold values from 0.05 to 5
- cutoff: int32 [32], P('lat'), may hold values from 4 to 359
- polar_flag: int32 [32], P('lat'), may hold values from 0 to 1, as said below
Outputs:
- adjoint_out: float32 [32, 1440, 128], P('lat', 'lon')
Inputs may be any that keep to these rules, and one draw needn't show every extreme that they name: polar_flag is 1 on a run of rows starting at row 0 and on a run ending at row 31, each of 1 to 8 rows and one of them exactly 8, and 0 elsewhere.
All inputs are finite; a program needn't handle non-finite values.
Results may differ from a plain program's by a relative error of at most 0.0003.
Values sent between devices are 32-bit elements; how exact they have to be, the bound alone decides.
No kernel may reach another device: no remote copies, remote signals or barrier semaphores. Data moves between devices by JAX's collectives and lax.ppermute only.
A program may use at most 64 MiB of HBM per device.

v0:
```python
from functools import partial
import math
import jax
import jax.numpy as jnp
from jax import lax
from jax.sharding import PartitionSpec as P

SUBSTEPS = 2


def partner(block, axis, stride):
    count = lax.axis_size(axis)
    route = []
    for low in range(count):
        high = low | 1 << stride
        if high != low and high < count:
            route += [(low, high), (high, low)]
    return lax.ppermute(block, axis, route)


def padded_2(value, sides, width, wrap):
    for axis, dim in sides:
        count, length = (lax.axis_size(axis), value.shape[dim])
        up = [(i, (i + 1) % count) for i in range(count if wrap else count - 1)]
        down = [(j, i) for i, j in up]
        last = lax.slice_in_dim(value, length - width, length, axis=dim)
        initial = lax.slice_in_dim(value, 0, width, axis=dim)
        before = lax.ppermute(last, axis, up)
        after = lax.ppermute(initial, axis, down)
        value = jnp.concatenate([before, value, after], axis=dim)
    return value


def edge_row(offset):
    row = [0.0] * 6
    row[offset + 2] += 7.0 / 12.0
    row[offset + 3] += 7.0 / 12.0
    row[offset + 1] -= 1.0 / 12.0
    row[offset + 4] -= 1.0 / 12.0
    return row


def flux_weights(courant):
    left_edge = edge_row(-1)
    middle_edge = edge_row(0)
    right_edge = edge_row(1)
    magnitude = jnp.abs(courant)
    result = []
    for position in range(6):
        cell_plus = 1.0 if position == 2 else 0.0
        cell_minus = 1.0 if position == 3 else 0.0
        delta_plus = middle_edge[position] - left_edge[position]
        curve_plus = 6.0 * (cell_plus - 0.5 * (left_edge[position] + middle_edge[position]))
        delta_minus = right_edge[position] - middle_edge[position]
        curve_minus = 6.0 * (cell_minus - 0.5 * (middle_edge[position] + right_edge[position]))
        bend = 1.0 - 2.0 * magnitude / 3.0
        forward_weight = middle_edge[position] - 0.5 * magnitude * (delta_plus - bend * curve_plus)
        backward_weight = middle_edge[position] + 0.5 * magnitude * (
            delta_minus + bend * curve_minus
        )
        result.append(courant * jnp.where(courant >= 0.0, forward_weight, backward_weight))
    return result


def spread_flux(field_ext, courant_ext, axis_dim):
    length = field_ext.shape[axis_dim]
    jump = lax.slice_in_dim(field_ext, 1, length, axis=axis_dim) - lax.slice_in_dim(
        field_ext, 0, length - 1, axis=axis_dim
    )
    weights = flux_weights(lax.slice_in_dim(courant_ext, 0, length - 1, axis=axis_dim))
    padding = [(0, 0)] * jump.ndim
    padding[axis_dim] = (3, 3)
    total = jnp.zeros(field_ext.shape, field_ext.dtype)
    for position in range(6):
        offset = position - 2
        term = jnp.pad(weights[position] * jump, padding)
        total = total + lax.slice_in_dim(term, 3 - offset, 3 - offset + length, axis=axis_dim)
    return total


def solve_setup(mixing, tracers):
    rows, cols, interfaces = mixing.shape
    levels = interfaces + 1
    coef = jnp.moveaxis(mixing, 2, 0)
    nothing = jnp.zeros_like(coef[:1])
    padded = jnp.concatenate([nothing, coef, nothing], axis=0)
    beneath = -padded[:levels]
    overlying = -padded[1:]
    central = 1.0 - beneath - overlying
    factor_prev = jnp.zeros_like(coef[0])
    factor_list = []
    divisor_list = []
    for level in range(levels):
        divisor = central[level] - beneath[level] * factor_prev
        factor = overlying[level] / divisor
        factor_list.append(factor)
        divisor_list.append(divisor)
        factor_prev = factor

    def spread_lanes(values):
        return jnp.broadcast_to(values[..., None], (levels, rows, cols, tracers)).reshape(
            levels, rows * cols * tracers
        )

    return (
        spread_lanes(beneath),
        spread_lanes(jnp.stack(factor_list)),
        spread_lanes(jnp.stack(divisor_list)),
    )


def vertical_apply(field, coeffs, levels):
    rows, cols, channels = field.shape
    tracers = channels // levels
    beneath, factors, divisors = coeffs
    stack = (
        field.reshape(rows, cols, levels, tracers)
        .transpose(2, 0, 1, 3)
        .reshape(levels, rows * cols * tracers)
    )
    partial_prev = jnp.zeros_like(stack[0])
    partials = []
    for level in range(levels):
        partial_now = (stack[level] - beneath[level] * partial_prev) / divisors[level]
        partials.append(partial_now)
        partial_prev = partial_now
    following = jnp.zeros_like(stack[0])
    solved = [None] * levels
    for level in range(levels - 1, -1, -1):
        current = partials[level] - factors[level] * following
        solved[level] = current
        following = current
    result = jnp.stack(solved).reshape(levels, rows, cols, tracers).transpose(1, 2, 0, 3)
    return result.reshape(rows, cols, channels)


def fourier_table(circle):
    halfway = circle // 2
    places = jnp.arange(circle, dtype=jnp.int32)
    columns = jnp.arange(circle, dtype=jnp.int32)
    waves = columns % halfway
    phase = places[:, None] * waves[None, :] % circle
    angle = phase.astype(jnp.float32) * (2.0 * math.pi / circle)
    return jnp.where(columns[None, :] < halfway, jnp.cos(angle), jnp.sin(angle))


def local_setting(cutoff, polar_flag, lat_rows, channels, row_index):
    lat_local = row_index // channels
    chosen = lat_local[:, None] == jnp.arange(lat_rows, dtype=jnp.int32)[None, :]
    row_cut = jnp.sum(jnp.where(chosen, cutoff[None, :], 0), axis=1)
    row_flag = jnp.sum(jnp.where(chosen, polar_flag[None, :], 0), axis=1)
    return (row_cut, row_flag)


def filter_rows(rows, setting, table):
    circles = lax.all_to_all(rows, "lon", split_axis=0, concat_axis=1, tiled=True)
    count = circles.shape[0]
    row_index = lax.axis_index("lon") * count + jnp.arange(count, dtype=jnp.int32)
    row_cut, row_flag = setting(row_index)
    circle = table.shape[0]
    halfway = table.shape[1] // 2
    columns = jnp.arange(table.shape[1], dtype=jnp.int32)
    waves = columns % halfway
    is_sine = columns >= halfway
    scaling = jnp.where(waves == 0, 1.0, 2.0) / circle
    spectra = jnp.dot(
        circles, table, precision=lax.Precision.HIGHEST, preferred_element_type=jnp.float32
    )
    active = (waves[None, :] <= row_cut[:, None]) & jnp.logical_not(is_sine & (waves == 0))[None, :]
    weighted = jnp.where(active, spectra * scaling[None, :], 0.0)
    smooth = lax.dot_general(
        weighted,
        table,
        (((1,), (1,)), ((), ())),
        precision=lax.Precision.HIGHEST,
        preferred_element_type=jnp.float32,
    )
    mixed = jnp.where((row_flag > 0)[:, None], smooth, circles)
    return lax.all_to_all(mixed, "lon", split_axis=1, concat_axis=0, tiled=True)


def widen(courant, tracers):
    return jnp.repeat(courant, tracers, axis=2)


def meridional_core(field_ext, courant_ext, lat_first, lat_total):
    length = field_ext.shape[0]
    face_index = lat_first - 3 + jnp.arange(length, dtype=jnp.int32)
    valid = (face_index >= 0) & (face_index <= lat_total - 2)
    courant_ext = jnp.where(valid[:, None, None], courant_ext, 0.0)
    full = spread_flux(field_ext, courant_ext, 0)
    result = field_ext[3 : length - 3] + full[3 : length - 3]
    ghosts = jnp.concatenate([full[0:3], full[length - 3 :]], axis=0)
    arrived = partner(ghosts, "lon", lax.axis_size("lon").bit_length() - 2)
    lat_index = lax.axis_index("lat")
    south = jnp.where(lat_index == 0, arrived[2::-1], 0.0)
    north = jnp.where(lat_index == lax.axis_size("lat") - 1, arrived[5:2:-1], 0.0)
    result = result.at[0:3].add(south)
    result = result.at[result.shape[0] - 3 :].add(north)
    return result


def on_device(sensitivity, courant_east, courant_north, mixing, cutoff, polar_flag):
    lat_rows, lon_cols, channels = sensitivity.shape
    levels = courant_east.shape[2]
    tracers = channels // levels
    lat_total = lat_rows * lax.axis_size("lat")
    lat_first = lax.axis_index("lat") * lat_rows
    table = fourier_table(lon_cols * lax.axis_size("lon"))
    coeffs = solve_setup(mixing, tracers)
    state = sensitivity
    for substep in range(SUBSTEPS):
        state = vertical_apply(state, coeffs, levels)
        rows = state.transpose(0, 2, 1).reshape(lat_rows * channels, lon_cols)
        setting = partial(local_setting, cutoff, polar_flag, lat_rows, channels)
        state = (
            filter_rows(rows, setting, table)
            .reshape(lat_rows, channels, lon_cols)
            .transpose(0, 2, 1)
        )
        stacked = jnp.concatenate([state, courant_north], axis=2)
        margin = padded_2(stacked, (("lat", 0),), 3, False)
        northward = meridional_core(
            margin[:, :, :channels], widen(margin[:, :, channels:], tracers), lat_first, lat_total
        )
        stacked = jnp.concatenate([northward, courant_east], axis=2)
        margin = padded_2(stacked, (("lon", 1),), 3, True)
        northward = margin[:, :, :channels]
        east_courant = widen(margin[:, :, channels:], tracers)
        state = northward[:, 3:-3] + spread_flux(northward, east_courant, 1)[:, 3:-3]
    return state


def solution(mesh):
    return jax.shard_map(
        on_device,
        mesh=mesh,
        in_specs=(
            P("lat", "lon", None),
            P("lat", "lon", None),
            P("lat", "lon", None),
            P("lat", "lon", None),
            P("lat"),
            P("lat"),
        ),
        out_specs=P("lat", "lon", None),
        check_vma=False,
    )
```

profile of v0, /device:TPU:9, one launch (start us, length us, event | category | flops | bytes accessed | tf_op | source)
XLA Modules:
  0.0 415.6 jit_solution(10514916888348440577)
XLA Ops:
  0.0 1.1 fusion.232
  2.2 0.7 fusion.169
  2.9 0.6 fusion.168
  3.6 0.6 fusion.170
  4.2 0.6 fusion.172
  4.8 0.6 fusion.174
  5.5 0.6 fusion.176
  6.2 1.6 constant_dynamic-update-slice_fusion.31
  8.7 1.2 copy.40
  9.9 4.0 all-to-all-start
  13.9 38.1 %sine_select_fusion.22 = f32[1440,1440]{1,0:T(8,128)} fusion(s32[1440]{0:T(1024)S(1)} %add_select_fusion.1, pred[1440]{0:T(1024)(128)(4,1)S(1)} %get-tuple-element.259), kind=kLoop, calls=%fused_computation.3.clone.3.clone.clone.clone.clone.clone | loop fusion | flops 20736000 | bytes 8301600 | tf_op jit(solution)/shard_map/dot_general | solution.py:166
  52.7 18.1 %fusion.18 = f32[128,1440]{0,1:T(8,128)S(1)} fusion(f32[128,1440]{0,1:T(8,128)S(1)} %bitcast.221, s32[1440]{0:T(1024)S(1)} %add_select_fusion.1, f32[1440]{0:T(1024)S(1)} %select_multiply_fusion, s32[128]{0:T(128)S(1)} %get-tuple-element.54, pred[1440]{0:T(1024)(128)(4,1)S(1)} %get-tuple-element.260, f32[1440,1440]{1,0:T(8,128)} %sine_select_fusion.22), kind=kOutput, calls=%fused_computation.35 | convolution fusion | flops 3185786880 | bytes 9782432 | tf_op jit(solution)/shard_map/dot_general | solution.py:166
  70.8 44.1 %fusion.15 = f32[128,1440]{0,1:T(8,128)S(1)} fusion(f32[128,1440]{0,1:T(8,128)S(1)} %bitcast.222, f32[128,1440]{0,1:T(8,128)S(1)} %fusion.18, s32[1440]{0:T(1024)S(1)} %add_select_fusion.1, pred[1440]{0:T(1024)(128)(4,1)S(1)} %get-tuple-element.259, pred[128]{0:T(512)(128)(4,1)S(1)} %broadcast_compare_fusion.3), kind=kOutput, calls=%fused_computation.32 | convolution fusion | flops 3205969920 | bytes 2219168 | tf_op jit(solution)/shard_map/dot_general | solution.py:171
  114.9 12.8 %all_to_all.58 = f32[128,4,360]{0,2,1:T(8,128)S(1)} all-to-all(f32[128,4,360]{0,2,1:T(8,128)S(1)} %bitcast.228), channel_id=1, replica_groups=mesh['lon'=4,'lat'=8] {'lon'}, dimensions={1} | all-to-all | bytes 1474560 | tf_op jit(solution)/shard_map/all_to_all | solution.py:179
  128.1 5.9 %collective-permute-start = (f32[3,360,160]{1,2,0:T(8,128)S(1)}, f32[3,360,160]{1,2,0:T(8,128)S(1)}, u32[]{:S(2)}, u32[]{:S(2)}) collective-permute-start(f32[3,360,160]{1,2,0:T(8,128)S(1)} %get-tuple-element.191), channel_id=1, source_target_pairs={{0,1},{1,2},{2,3},{3,4},{4,5},{5,6},{6,7},{8,9},{9,10},{10,11},{11... | collective-permute-start | bytes 2073608 | tf_op jit(solution)/shard_map/ppermute | solution.py:28
  134.1 1.9 collective-permute-start.1
  136.0 0.6 compare_and_fusion.1
  136.6 5.7 %collective-permute-done = f32[3,360,160]{1,2,0:T(8,128)S(1)} collective-permute-done((f32[3,360,160]{1,2,0:T(8,128)S(1)}, f32[3,360,160]{1,2,0:T(8,128)S(1)}, u32[]{:S(2)}, u32[]{:S(2)}) %collective-permute-start) | collective-permute-done | bytes 691232 | tf_op jit(solution)/shard_map/ppermute | solution.py:28
  142.2 0.9 copy-done.7
  143.1 3.9 collective-permute-done.1
  146.9 1.5 fusion.12
  148.5 1.6 broadcast_in_dim.435
  150.1 2.9 reshape.8039
  153.0 2.7 multiply_multiply_fusion.6
  155.7 3.2 multiply_multiply_fusion.7
  159.0 0.6 fusion.23
  159.6 1.2 copy-done.2
  161.3 0.6 collective-permute-start.2
  161.9 1.2 slice_add_fusion.11
  163.1 23.5 %collective-permute-done.2 = f32[6,360,128]{2,1,0:T(8,128)} collective-permute-done((f32[6,360,128]{2,1,0:T(8,128)S(1)}, f32[6,360,128]{2,1,0:T(8,128)}, u32[]{:S(2)}, u32[]{:S(2)}) %collective-permute-start.2) | collective-permute-done | bytes 1105952 | tf_op jit(solution)/shard_map/ppermute | solution.py:18
  186.6 1.3 fusion.231
  188.7 0.6 copy-done.5
  190.0 2.1 collective-permute-start.4
  192.1 7.9 %collective-permute-done.3 = f32[4,3,160]{1,2,0:T(8,128)S(1)} collective-permute-done((f32[4,3,160]{1,2,0:T(8,128)S(1)}, f32[4,3,160]{1,2,0:T(8,128)S(1)}, u32[]{:S(2)}, u32[]{:S(2)}) %collective-permute-start.3) | collective-permute-done | bytes 7712 | tf_op jit(solution)/shard_map/ppermute | solution.py:28
  200.0 6.3 %collective-permute-done.4 = f32[4,3,160]{1,2,0:T(8,128)S(1)} collective-permute-done((f32[4,3,160]{1,2,0:T(8,128)S(1)}, f32[4,3,160]{1,2,0:T(8,128)S(1)}, u32[]{:S(2)}, u32[]{:S(2)}) %collective-permute-start.4) | collective-permute-done | bytes 7712 | tf_op jit(solution)/shard_map/ppermute | solution.py:29
  207.5 1.4 multiply_multiply_fusion.22
  210.6 1.3 fusion.38
  212.8 1.6 constant_dynamic-update-slice_fusion.63
  215.0 1.2 copy.48
  216.2 4.0 all-to-all-start.2
  220.2 38.1 %sine_select_fusion.21 = f32[1440,1440]{1,0:T(8,128)} fusion(s32[1440]{0:T(1024)S(1)} %copy-done.18, pred[1440]{0:T(1024)(128)(4,1)S(1)} %copy-done.94), kind=kLoop, calls=%fused_computation.3.clone.1.clone.clone.clone.clone.clone.1 | loop fusion | flops 20736000 | bytes 8301600 | tf_op jit(solution)/shard_map/dot_general | solution.py:166
  258.4 18.1 %fusion.17 = f32[128,1440]{0,1:T(8,128)S(1)} fusion(f32[128,1440]{0,1:T(8,128)S(1)} %bitcast.223, s32[1440]{0:T(1024)S(1)} %copy-done.18, f32[1440]{0:T(1024)S(1)} %copy-done.52, s32[128]{0:T(128)S(1)} %copy-done.98, pred[1440]{0:T(1024)(128)(4,1)S(1)} %copy-done.92, f32[1440,1440]{1,0:T(8,128)} %sine_select_fusion.21), kind=kOutput, calls=%fused_computation.34 | convolution fusion | flops 3185786880 | bytes 9782432 | tf_op jit(solution)/shard_map/dot_general | solution.py:166
  276.5 44.1 %fusion.16 = f32[128,1440]{0,1:T(8,128)S(1)} fusion(f32[128,1440]{0,1:T(8,128)S(1)} %bitcast.224, f32[128,1440]{0,1:T(8,128)S(1)} %fusion.17, s32[1440]{0:T(1024)S(1)} %copy-done.18, pred[1440]{0:T(1024)(128)(4,1)S(1)} %copy-done.94, pred[128]{0:T(512)(128)(4,1)S(1)} %copy-done.102), kind=kOutput, calls=%fused_computation.33 | convolution fusion | flops 3205969920 | bytes 2219168 | tf_op jit(solution)/shard_map/dot_general | solution.py:171
  320.6 12.7 %all_to_all.59 = f32[128,4,360]{0,2,1:T(8,128)S(1)} all-to-all(f32[128,4,360]{0,2,1:T(8,128)S(1)} %bitcast.227), channel_id=1, replica_groups=mesh['lon'=4,'lat'=8] {'lon'}, dimensions={1} | all-to-all | bytes 1474560 | tf_op jit(solution)/shard_map/all_to_all | solution.py:179
  333.7 5.9 %collective-permute-start.5 = (f32[3,360,160]{1,2,0:T(8,128)S(1)}, f32[3,360,160]{1,2,0:T(8,128)S(1)}, u32[]{:S(2)}, u32[]{:S(2)}) collective-permute-start(f32[3,360,160]{1,2,0:T(8,128)S(1)} %get-tuple-element.187), channel_id=1, source_target_pairs={{0,1},{1,2},{2,3},{3,4},{4,5},{5,6},{6,7},{8,9},{9,10},{10,11},{11... | collective-permute-start | bytes 2073608 | tf_op jit(solution)/shard_map/ppermute | solution.py:28
  339.5 1.9 collective-permute-start.6
  341.5 6.2 %collective-permute-done.5 = f32[3,360,160]{1,2,0:T(8,128)S(1)} collective-permute-done((f32[3,360,160]{1,2,0:T(8,128)S(1)}, f32[3,360,160]{1,2,0:T(8,128)S(1)}, u32[]{:S(2)}, u32[]{:S(2)}) %collective-permute-start.5) | collective-permute-done | bytes 691232 | tf_op jit(solution)/shard_map/ppermute | solution.py:28
  347.7 4.6 %collective-permute-done.6 = f32[3,360,160]{1,2,0:T(8,128)S(1)} collective-permute-done((f32[3,360,160]{1,2,0:T(8,128)S(1)}, f32[3,360,160]{1,2,0:T(8,128)S(1)}, u32[]{:S(2)}, u32[]{:S(2)}) %collective-permute-start.6) | collective-permute-done | bytes 691232 | tf_op jit(solution)/shard_map/ppermute | solution.py:29
  352.5 1.6 broadcast_in_dim.439
  354.2 2.9 reshape.8043
  357.1 2.7 multiply_multiply_fusion
  359.7 3.2 multiply_multiply_fusion.1
  363.0 0.6 fusion.28
  363.6 1.2 copy-done.3
  365.4 0.6 collective-permute-start.7
  365.9 1.2 slice_add_fusion.5
  367.1 23.5 %collective-permute-done.7 = f32[6,360,128]{2,1,0:T(8,128)S(1)} collective-permute-done((f32[6,360,128]{2,1,0:T(8,128)S(1)}, f32[6,360,128]{2,1,0:T(8,128)S(1)}, u32[]{:S(2)}, u32[]{:S(2)}) %collective-permute-start.7) | collective-permute-done | bytes 1105952 | tf_op jit(solution)/shard_map/ppermute | solution.py:18
  391.5 0.6 copy-done.6
  392.8 1.9 collective-permute-start.9
  394.7 8.0 %collective-permute-done.8 = f32[4,3,160]{1,2,0:T(8,128)S(1)} collective-permute-done((f32[4,3,160]{1,2,0:T(8,128)S(1)}, f32[4,3,160]{1,2,0:T(8,128)S(1)}, u32[]{:S(2)}, u32[]{:S(2)}) %collective-permute-start.8) | collective-permute-done | bytes 7712 | tf_op jit(solution)/shard_map/ppermute | solution.py:28
  402.7 6.3 %collective-permute-done.9 = f32[4,3,160]{1,2,0:T(8,128)S(1)} collective-permute-done((f32[4,3,160]{1,2,0:T(8,128)S(1)}, f32[4,3,160]{1,2,0:T(8,128)S(1)}, u32[]{:S(2)}, u32[]{:S(2)}) %collective-permute-start.9) | collective-permute-done | bytes 7712 | tf_op jit(solution)/shard_map/ppermute | solution.py:29
  410.2 1.4 multiply_multiply_fusion.16
  412.9 1.3 fusion.37
  414.2 1.1 copy.55
  (324 shorter events, 13.2 us)
Async XLA Ops:
  1.2 4.9 %copy-start.53 = (f32[4,360]{1,0:T(4,128)}, f32[4,360]{1,0:T(4,128)S(1)}, u32[]{:S(2)}) copy-start(f32[4,360]{1,0:T(4,128)S(1)} %get-tuple-element.243) | copy-start | bytes 17284
  1.2 4.9 %copy-start.55 = (f32[4,360]{1,0:T(4,128)}, f32[4,360]{1,0:T(4,128)S(1)}, u32[]{:S(2)}) copy-start(f32[4,360]{1,0:T(4,128)S(1)} %get-tuple-element.244) | copy-start | bytes 17284
  1.2 4.9 %copy-start.57 = (f32[4,360]{1,0:T(4,128)}, f32[4,360]{1,0:T(4,128)S(1)}, u32[]{:S(2)}) copy-start(f32[4,360]{1,0:T(4,128)S(1)} %get-tuple-element.245) | copy-start | bytes 17284
  1.2 4.9 %copy-start.59 = (f32[4,360]{1,0:T(4,128)}, f32[4,360]{1,0:T(4,128)S(1)}, u32[]{:S(2)}) copy-start(f32[4,360]{1,0:T(4,128)S(1)} %get-tuple-element.246) | copy-start | bytes 17284
  1.2 4.9 %copy-start.61 = (f32[4,360]{1,0:T(4,128)}, f32[4,360]{1,0:T(4,128)S(1)}, u32[]{:S(2)}) copy-start(f32[4,360]{1,0:T(4,128)S(1)} %get-tuple-element.247) | copy-start | bytes 17284
  1.2 4.9 %copy-start.63 = (f32[4,360]{1,0:T(4,128)}, f32[4,360]{1,0:T(4,128)S(1)}, u32[]{:S(2)}) copy-start(f32[4,360]{1,0:T(4,128)S(1)} %get-tuple-element.248) | copy-start | bytes 17284
  1.2 4.9 %copy-start.65 = (f32[4,360]{1,0:T(4,128)}, f32[4,360]{1,0:T(4,128)S(1)}, u32[]{:S(2)}) copy-start(f32[4,360]{1,0:T(4,128)S(1)} %get-tuple-element.249) | copy-start | bytes 17284
  1.2 4.9 %copy-start.67 = (f32[4,360]{1,0:T(4,128)}, f32[4,360]{1,0:T(4,128)S(1)}, u32[]{:S(2)}) copy-start(f32[4,360]{1,0:T(4,128)S(1)} %get-tuple-element.250) | copy-start | bytes 17284
  1.2 4.9 %copy-start.69 = (f32[4,360]{1,0:T(4,128)}, f32[4,360]{1,0:T(4,128)S(1)}, u32[]{:S(2)}) copy-start(f32[4,360]{1,0:T(4,128)S(1)} %get-tuple-element.251) | copy-start | bytes 17284
  1.3 4.9 %copy-start.71 = (f32[4,360]{1,0:T(4,128)}, f32[4,360]{1,0:T(4,128)S(1)}, u32[]{:S(2)}) copy-start(f32[4,360]{1,0:T(4,128)S(1)} %get-tuple-element.252) | copy-start | bytes 17284
  1.3 4.9 %copy-start.73 = (f32[4,360]{1,0:T(4,128)}, f32[4,360]{1,0:T(4,128)S(1)}, u32[]{:S(2)}) copy-start(f32[4,360]{1,0:T(4,128)S(1)} %get-tuple-element.253) | copy-start | bytes 17284
  1.3 4.9 %copy-start.75 = (f32[4,360]{1,0:T(4,128)}, f32[4,360]{1,0:T(4,128)S(1)}, u32[]{:S(2)}) copy-start(f32[4,360]{1,0:T(4,128)S(1)} %get-tuple-element.254) | copy-start | bytes 17284
  1.3 4.9 %copy-start.77 = (f32[4,360]{1,0:T(4,128)}, f32[4,360]{1,0:T(4,128)S(1)}, u32[]{:S(2)}) copy-start(f32[4,360]{1,0:T(4,128)S(1)} %get-tuple-element.255) | copy-start | bytes 17284
  1.3 4.9 %copy-start.79 = (f32[4,360]{1,0:T(4,128)}, f32[4,360]{1,0:T(4,128)S(1)}, u32[]{:S(2)}) copy-start(f32[4,360]{1,0:T(4,128)S(1)} %get-tuple-element.256) | copy-start | bytes 17284
  1.7 6.1 %copy-start.19 = (f32[1,4,360]{2,1,0:T(4,128)}, f32[1,4,360]{2,1,0:T(4,128)S(1)}, u32[]{:S(2)}) copy-start(f32[1,4,360]{2,1,0:T(4,128)S(1)} %get-tuple-element.127) | copy-start | bytes 17284
  1.7 6.1 %copy-start.21 = (f32[1,4,360]{2,1,0:T(4,128)}, f32[1,4,360]{2,1,0:T(4,128)S(1)}, u32[]{:S(2)}) copy-start(f32[1,4,360]{2,1,0:T(4,128)S(1)} %get-tuple-element.129) | copy-start | bytes 17284
  1.7 6.1 %copy-start.23 = (f32[1,4,360]{2,1,0:T(4,128)}, f32[1,4,360]{2,1,0:T(4,128)S(1)}, u32[]{:S(2)}) copy-start(f32[1,4,360]{2,1,0:T(4,128)S(1)} %get-tuple-element.131) | copy-start | bytes 17284
  1.7 6.1 %copy-start.25 = (f32[1,4,360]{2,1,0:T(4,128)}, f32[1,4,360]{2,1,0:T(4,128)S(1)}, u32[]{:S(2)}) copy-start(f32[1,4,360]{2,1,0:T(4,128)S(1)} %get-tuple-element.133) | copy-start | bytes 17284
  1.8 6.1 %copy-start.27 = (f32[1,4,360]{2,1,0:T(4,128)}, f32[1,4,360]{2,1,0:T(4,128)S(1)}, u32[]{:S(2)}) copy-start(f32[1,4,360]{2,1,0:T(4,128)S(1)} %get-tuple-element.135) | copy-start | bytes 17284
  1.8 6.1 %copy-start.29 = (f32[1,4,360]{2,1,0:T(4,128)}, f32[1,4,360]{2,1,0:T(4,128)S(1)}, u32[]{:S(2)}) copy-start(f32[1,4,360]{2,1,0:T(4,128)S(1)} %get-tuple-element.137) | copy-start | bytes 17284
  1.8 6.1 %copy-start.31 = (f32[1,4,360]{2,1,0:T(4,128)}, f32[1,4,360]{2,1,0:T(4,128)S(1)}, u32[]{:S(2)}) copy-start(f32[1,4,360]{2,1,0:T(4,128)S(1)} %get-tuple-element.139) | copy-start | bytes 17284
  1.8 6.1 %copy-start.33 = (f32[1,4,360]{2,1,0:T(4,128)}, f32[1,4,360]{2,1,0:T(4,128)S(1)}, u32[]{:S(2)}) copy-start(f32[1,4,360]{2,1,0:T(4,128)S(1)} %get-tuple-element.141) | copy-start | bytes 17284
  1.8 6.1 %copy-start.35 = (f32[1,4,360]{2,1,0:T(4,128)}, f32[1,4,360]{2,1,0:T(4,128)S(1)}, u32[]{:S(2)}) copy-start(f32[1,4,360]{2,1,0:T(4,128)S(1)} %get-tuple-element.143) | copy-start | bytes 17284
  1.8 6.1 %copy-start.37 = (f32[1,4,360]{2,1,0:T(4,128)}, f32[1,4,360]{2,1,0:T(4,128)S(1)}, u32[]{:S(2)}) copy-start(f32[1,4,360]{2,1,0:T(4,128)S(1)} %get-tuple-element.145) | copy-start | bytes 17284
  1.8 6.1 %copy-start.39 = (f32[1,4,360]{2,1,0:T(4,128)}, f32[1,4,360]{2,1,0:T(4,128)S(1)}, u32[]{:S(2)}) copy-start(f32[1,4,360]{2,1,0:T(4,128)S(1)} %get-tuple-element.147) | copy-start | bytes 17284
  1.8 6.1 %copy-start.41 = (f32[1,4,360]{2,1,0:T(4,128)}, f32[1,4,360]{2,1,0:T(4,128)S(1)}, u32[]{:S(2)}) copy-start(f32[1,4,360]{2,1,0:T(4,128)S(1)} %get-tuple-element.149) | copy-start | bytes 17284
  1.8 6.1 %copy-start.43 = (f32[1,4,360]{2,1,0:T(4,128)}, f32[1,4,360]{2,1,0:T(4,128)S(1)}, u32[]{:S(2)}) copy-start(f32[1,4,360]{2,1,0:T(4,128)S(1)} %get-tuple-element.151) | copy-start | bytes 17284
  1.8 6.1 %copy-start.45 = (f32[1,4,360]{2,1,0:T(4,128)}, f32[1,4,360]{2,1,0:T(4,128)S(1)}, u32[]{:S(2)}) copy-start(f32[1,4,360]{2,1,0:T(4,128)S(1)} %get-tuple-element.153) | copy-start | bytes 17284
  1.9 6.1 %copy-start.47 = (f32[1,4,360]{2,1,0:T(4,128)}, f32[1,4,360]{2,1,0:T(4,128)S(1)}, u32[]{:S(2)}) copy-start(f32[1,4,360]{2,1,0:T(4,128)S(1)} %get-tuple-element.155) | copy-start | bytes 17284
  1.9 6.1 %copy-start.49 = (f32[1,4,360]{2,1,0:T(4,128)}, f32[1,4,360]{2,1,0:T(4,128)S(1)}, u32[]{:S(2)}) copy-start(f32[1,4,360]{2,1,0:T(4,128)S(1)} %get-tuple-element.156) | copy-start | bytes 17284
  1.9 6.1 %copy-start.15 = (f32[1,4,360]{2,1,0:T(4,128)}, f32[1,4,360]{2,1,0:T(4,128)S(1)}, u32[]{:S(2)}) copy-start(f32[1,4,360]{2,1,0:T(4,128)S(1)} %get-tuple-element.154) | copy-start | bytes 17284
  1.9 6.2 %copy-start.13 = (f32[1,4,360]{2,1,0:T(4,128)}, f32[1,4,360]{2,1,0:T(4,128)S(1)}, u32[]{:S(2)}) copy-start(f32[1,4,360]{2,1,0:T(4,128)S(1)} %get-tuple-element.152) | copy-start | bytes 17284
  1.9 6.2 %copy-start.11 = (f32[1,4,360]{2,1,0:T(4,128)}, f32[1,4,360]{2,1,0:T(4,128)S(1)}, u32[]{:S(2)}) copy-start(f32[1,4,360]{2,1,0:T(4,128)S(1)} %get-tuple-element.150) | copy-start | bytes 17284
  1.9 6.3 %copy-start.9 = (f32[1,4,360]{2,1,0:T(4,128)}, f32[1,4,360]{2,1,0:T(4,128)S(1)}, u32[]{:S(2)}) copy-start(f32[1,4,360]{2,1,0:T(4,128)S(1)} %get-tuple-element.148) | copy-start | bytes 17284
  2.9 5.2 %copy-start.81 = (f32[4,360]{1,0:T(4,128)}, f32[4,360]{1,0:T(4,128)S(1)}, u32[]{:S(2)}) copy-start(f32[4,360]{1,0:T(4,128)S(1)} %get-tuple-element.223) | copy-start | bytes 17284
  2.9 5.2 %copy-start.83 = (f32[4,360]{1,0:T(4,128)}, f32[4,360]{1,0:T(4,128)S(1)}, u32[]{:S(2)}) copy-start(f32[4,360]{1,0:T(4,128)S(1)} %get-tuple-element.224) | copy-start | bytes 17284
  2.9 5.2 %copy-start.85 = (f32[4,360]{1,0:T(4,128)}, f32[4,360]{1,0:T(4,128)S(1)}, u32[]{:S(2)}) copy-start(f32[4,360]{1,0:T(4,128)S(1)} %get-tuple-element.230) | copy-start | bytes 17284
  2.9 5.2 %copy-start.87 = (f32[4,360]{1,0:T(4,128)}, f32[4,360]{1,0:T(4,128)S(1)}, u32[]{:S(2)}) copy-start(f32[4,360]{1,0:T(4,128)S(1)} %get-tuple-element.231) | copy-start | bytes 17284
  2.9 5.2 %copy-start.89 = (f32[4,360]{1,0:T(4,128)}, f32[4,360]{1,0:T(4,128)S(1)}, u32[]{:S(2)}) copy-start(f32[4,360]{1,0:T(4,128)S(1)} %get-tuple-element.232) | copy-start | bytes 17284
  9.9 42.3 %all-to-all-start = ((f32[4,128,360]{1,2,0:T(8,128)}), f32[4,128,360]{1,2,0:T(8,128)S(1)}, u32[]{:S(2)}, u32[]{:S(2)}) async-start(f32[4,128,360]{1,2,0:T(8,128)} %copy.40), calls=%async_computation | async-start | bytes 1474560 | tf_op jit(solution)/shard_map/all_to_all | solution.py:156
  13.8 57.0 %copy-start.17 = (s32[1440]{0:T(1024)}, s32[1440]{0:T(1024)S(1)}, u32[]{:S(2)}) copy-start(s32[1440]{0:T(1024)S(1)} %add_select_fusion.1) | copy-start | bytes 17284
  13.9 38.3 %copy-start.91 = (pred[1440]{0:T(1024)(128)(4,1)}, pred[1440]{0:T(1024)(128)(4,1)S(1)}, u32[]{:S(2)}) copy-start(pred[1440]{0:T(1024)(128)(4,1)S(1)} %get-tuple-element.260) | copy-start | bytes 4324
  13.9 56.9 %copy-start.93 = (pred[1440]{0:T(1024)(128)(4,1)}, pred[1440]{0:T(1024)(128)(4,1)S(1)}, u32[]{:S(2)}) copy-start(pred[1440]{0:T(1024)(128)(4,1)S(1)} %get-tuple-element.259) | copy-start | bytes 4324
  13.9 38.1 %copy-start.99 = (s32[4]{0:T(128)S(1)}, s32[4]{0:T(128)}, u32[]{:S(2)}) copy-start(s32[4]{0:T(128)} %param.19) | copy-start | bytes 52
  13.9 38.1 %copy-start.100 = (s32[4]{0:T(128)S(1)}, s32[4]{0:T(128)}, u32[]{:S(2)}) copy-start(s32[4]{0:T(128)} %param.18) | copy-start | bytes 52
  52.2 18.6 %copy-start.101 = (pred[128]{0:T(512)(128)(4,1)}, pred[128]{0:T(512)(128)(4,1)S(1)}, u32[]{:S(2)}) copy-start(pred[128]{0:T(512)(128)(4,1)S(1)} %broadcast_compare_fusion.3) | copy-start | bytes 388
  114.9 13.1 %copy-start.4 = (f32[4,360,32]{1,2,0:T(8,128)S(1)}, f32[4,360,32]{1,2,0:T(8,128)}, u32[]{:S(2)}) copy-start(f32[4,360,32]{1,2,0:T(8,128)} %param.16) | copy-start | bytes 552964
  128.1 14.1 %collective-permute-start = (f32[3,360,160]{1,2,0:T(8,128)S(1)}, f32[3,360,160]{1,2,0:T(8,128)S(1)}, u32[]{:S(2)}, u32[]{:S(2)}) collective-permute-start(f32[3,360,160]{1,2,0:T(8,128)S(1)} %get-tuple-element.191), channel_id=1, source_target_pairs={{0,1},{1,2},{2,3},{3,4},{4,5},{5,6},{6,7},{8,9},{9,10},{10,11},{11... | collective-permute-start | bytes 2073608 | tf_op jit(solution)/shard_map/ppermute | solution.py:28
  134.1 12.9 %collective-permute-start.1 = (f32[3,360,160]{1,2,0:T(8,128)S(1)}, f32[3,360,160]{1,2,0:T(8,128)}, u32[]{:S(2)}, u32[]{:S(2)}) collective-permute-start(f32[3,360,160]{1,2,0:T(8,128)S(1)} %get-tuple-element.192), channel_id=1, source_target_pairs={{1,0},{2,1},{3,2},{4,3},{5,4},{6,5},{7,6},{9,8},{10,9},{11,10},{12... | collective-permute-start | bytes 2073608 | tf_op jit(solution)/shard_map/ppermute | solution.py:29
  161.3 25.3 %collective-permute-start.2 = (f32[6,360,128]{2,1,0:T(8,128)S(1)}, f32[6,360,128]{2,1,0:T(8,128)}, u32[]{:S(2)}, u32[]{:S(2)}) collective-permute-start(f32[6,360,128]{2,1,0:T(8,128)S(1)} %copy.42), channel_id=1, source_target_pairs={{0,16},{16,0},{8,24},{24,8},{1,17},{17,1},{9,25},{25,9},{2,18},{18... | collective-permute-start | bytes 3317768 | tf_op jit(solution)/shard_map/ppermute | solution.py:18
  189.5 10.5 %collective-permute-start.3 = (f32[4,3,160]{1,2,0:T(8,128)S(1)}, f32[4,3,160]{1,2,0:T(8,128)S(1)}, u32[]{:S(2)}, u32[]{:S(2)}) collective-permute-start(f32[4,3,160]{1,2,0:T(8,128)S(1)} %get-tuple-element.189), channel_id=1, source_target_pairs={{0,8},{8,16},{16,24},{24,0},{1,9},{9,17},{17,25},{25,1},{2,10},{10... | collective-permute-start | bytes 23048 | tf_op jit(solution)/shard_map/ppermute | solution.py:28
  190.0 16.3 %collective-permute-start.4 = (f32[4,3,160]{1,2,0:T(8,128)S(1)}, f32[4,3,160]{1,2,0:T(8,128)S(1)}, u32[]{:S(2)}, u32[]{:S(2)}) collective-permute-start(f32[4,3,160]{1,2,0:T(8,128)S(1)} %get-tuple-element.190), channel_id=1, source_target_pairs={{8,0},{16,8},{24,16},{0,24},{9,1},{17,9},{25,17},{1,25},{10,2},{18... | collective-permute-start | bytes 23048 | tf_op jit(solution)/shard_map/ppermute | solution.py:29
  214.9 5.3 %copy-start.18 = (s32[1440]{0:T(1024)S(1)}, s32[1440]{0:T(1024)}, u32[]{:S(2)}) copy-start(s32[1440]{0:T(1024)} %copy-done.17) | copy-start | bytes 17284
  214.9 5.3 %copy-start.94 = (pred[1440]{0:T(1024)(128)(4,1)S(1)}, pred[1440]{0:T(1024)(128)(4,1)}, u32[]{:S(2)}) copy-start(pred[1440]{0:T(1024)(128)(4,1)} %copy-done.93) | copy-start | bytes 4324
  216.2 42.1 %all-to-all-start.2 = ((f32[4,128,360]{1,2,0:T(8,128)}), f32[4,128,360]{1,2,0:T(8,128)S(1)}, u32[]{:S(2)}, u32[]{:S(2)}) async-start(f32[4,128,360]{1,2,0:T(8,128)} %copy.48), calls=%async_computation.2 | async-start | bytes 1474560 | tf_op jit(solution)/shard_map/all_to_all | solution.py:156
  220.2 38.1 %copy-start.52 = (f32[1440]{0:T(1024)S(1)}, f32[1440]{0:T(1024)}, u32[]{:S(2)}) copy-start(f32[1440]{0:T(1024)} %copy-done.51) | copy-start | bytes 17284
  220.2 38.1 %copy-start.92 = (pred[1440]{0:T(1024)(128)(4,1)S(1)}, pred[1440]{0:T(1024)(128)(4,1)}, u32[]{:S(2)}) copy-start(pred[1440]{0:T(1024)(128)(4,1)} %copy-done.91) | copy-start | bytes 4324
  220.2 38.1 %copy-start.98 = (s32[128]{0:T(128)S(1)}, s32[128]{0:T(128)}, u32[]{:S(2)}) copy-start(s32[128]{0:T(128)} %copy-done.97) | copy-start | bytes 1540
  258.3 18.1 %copy-start.102 = (pred[128]{0:T(512)(128)(4,1)S(1)}, pred[128]{0:T(512)(128)(4,1)}, u32[]{:S(2)}) copy-start(pred[128]{0:T(512)(128)(4,1)} %copy-done.101) | copy-start | bytes 388
  333.7 14.0 %collective-permute-start.5 = (f32[3,360,160]{1,2,0:T(8,128)S(1)}, f32[3,360,160]{1,2,0:T(8,128)S(1)}, u32[]{:S(2)}, u32[]{:S(2)}) collective-permute-start(f32[3,360,160]{1,2,0:T(8,128)S(1)} %get-tuple-element.187), channel_id=1, source_target_pairs={{0,1},{1,2},{2,3},{3,4},{4,5},{5,6},{6,7},{8,9},{9,10},{10,11},{11... | collective-permute-start | bytes 2073608 | tf_op jit(solution)/shard_map/ppermute | solution.py:28
  339.5 12.8 %collective-permute-start.6 = (f32[3,360,160]{1,2,0:T(8,128)S(1)}, f32[3,360,160]{1,2,0:T(8,128)S(1)}, u32[]{:S(2)}, u32[]{:S(2)}) collective-permute-start(f32[3,360,160]{1,2,0:T(8,128)S(1)} %get-tuple-element.188), channel_id=1, source_target_pairs={{1,0},{2,1},{3,2},{4,3},{5,4},{6,5},{7,6},{9,8},{10,9},{11,10},{12... | collective-permute-start | bytes 2073608 | tf_op jit(solution)/shard_map/ppermute | solution.py:29
  365.4 25.3 %collective-permute-start.7 = (f32[6,360,128]{2,1,0:T(8,128)S(1)}, f32[6,360,128]{2,1,0:T(8,128)S(1)}, u32[]{:S(2)}, u32[]{:S(2)}) collective-permute-start(f32[6,360,128]{2,1,0:T(8,128)S(1)} %copy.50), channel_id=1, source_target_pairs={{0,16},{16,0},{8,24},{24,8},{1,17},{17,1},{9,25},{25,9},{2,18},{18... | collective-permute-start | bytes 3317768 | tf_op jit(solution)/shard_map/ppermute | solution.py:18
  392.3 10.4 %collective-permute-start.8 = (f32[4,3,160]{1,2,0:T(8,128)S(1)}, f32[4,3,160]{1,2,0:T(8,128)S(1)}, u32[]{:S(2)}, u32[]{:S(2)}) collective-permute-start(f32[4,3,160]{1,2,0:T(8,128)S(1)} %get-tuple-element.185), channel_id=1, source_target_pairs={{0,8},{8,16},{16,24},{24,0},{1,9},{9,17},{17,25},{25,1},{2,10},{10... | collective-permute-start | bytes 23048 | tf_op jit(solution)/shard_map/ppermute | solution.py:28
  392.8 16.2 %collective-permute-start.9 = (f32[4,3,160]{1,2,0:T(8,128)S(1)}, f32[4,3,160]{1,2,0:T(8,128)S(1)}, u32[]{:S(2)}, u32[]{:S(2)}) collective-permute-start(f32[4,3,160]{1,2,0:T(8,128)S(1)} %get-tuple-element.186), channel_id=1, source_target_pairs={{8,0},{16,8},{24,16},{0,24},{9,1},{17,9},{25,17},{1,25},{10,2},{18... | collective-permute-start | bytes 23048 | tf_op jit(solution)/shard_map/ppermute | solution.py:29
  (51 other events, 105.6 us)
where the time goes:
time: 419 us; the launch traced here: 416 us
  matrix products  124 us (30%)
  other arithmetic  110 us (26%)
  waiting for transfers between devices  95.9 us (23%)
  starting transfers between devices  29.8 us (7%)
  local copies, waits for them, and re-layouts  27.4 us (7%)
  blocking collectives  25.5 us (6%)
    dot_general x2, matrix products, filter_rows(): lax.dot_general(weighted, table, (((1,), (1,)), ((), ())), precision=lax....  88.2 us
    dot_general x2, other arithmetic, filter_rows(): jnp.dot(circles, table, precision=lax.Precision.HIGHEST, preferred_elemen...  76.2 us
    ppermute x2, waiting for transfers between devices, partner(): return lax.ppermute(block, axis, route)  47 us
    dot_general x2, matrix products, filter_rows(): jnp.dot(circles, table, precision=lax.Precision.HIGHEST, preferred_elemen...  36.1 us
    ppermute x4, waiting for transfers between devices, padded_2(): before = lax.ppermute(last, axis, up)  27.7 us
    all_to_all x2, blocking collectives, filter_rows(): return lax.all_to_all(mixed, 'lon', split_axis=1, concat_axis=0, tiled=True)  25.5 us
    ppermute x4, waiting for transfers between devices, padded_2(): after = lax.ppermute(initial, axis, down)  21.1 us
    mul x8, other arithmetic, spread_flux(): term = jnp.pad(weights[position] * jump, padding)  15.4 us
  transfers between devices with their start and end apart: 12, of which 10 were waited for; matrix products, arithmetic and copies ran while one was open for 19% of the time, Pallas kernels for 0%

commit v1 on v0

--- a/solution.py
+++ b/solution.py
@@ -176,7 +176,10 @@
         preferred_element_type=jnp.float32,
     )
     mixed = jnp.where((row_flag > 0)[:, None], smooth, circles)
-    return lax.all_to_all(mixed, "lon", split_axis=1, concat_axis=0, tiled=True)
+    return jnp.concatenate(
+        lax.all_to_all(jnp.stack(jnp.split(mixed, lax.axis_size("lon"), axis=1)), "lon", 0, 0),
+        axis=0,
+    )
 
 
 def widen(courant, tracers):

time: 419 us -> 430 us (1.026)
  local copies, waits for them, and re-layouts: 27.4 us -> 58.9 us
  waiting for transfers between devices: 95.9 us -> 77.8 us
  blocking collectives: 25.5 us -> 12.8 us
  other arithmetic: 110 us -> 116 us
    ppermute x4, waiting for transfers between devices: 27.7 us -> 11 us  [padded_2(): before = lax.ppermute(last, axis, up)]
    all_to_all x2 -> x1, blocking collectives: 25.5 us -> 12.8 us  [filter_rows(): lax.all_to_all(jnp.stack(jnp.split(mixed, lax.axis_size('lon'), axis=1)),...]
    slice x0 -> x6, local copies, waits for them, and re-layouts: none -> 12.6 us  [the longest x2 5.77 us: spread_flux(): lax.slice_in_dim(courant_ext, 0, length - 1, axis=axis_dim)]
    ppermute x4, waiting for transfers between devices: 21.1 us -> 9.83 us  [padded_2(): after = lax.ppermute(initial, axis, down)]
    all_to_all x0 -> x1, waiting for transfers between devices: none -> 9.48 us  [filter_rows(): lax.all_to_all(jnp.stack(jnp.split(mixed, lax.axis_size('lon'), axis=1)),...]
    ppermute x0 -> x4, local copies, waits for them, and re-layouts: none -> 8.9 us  [the longest x2 4.95 us: padded_2(): after = lax.ppermute(initial, axis, down)]
    unnamed x241 -> x179, local copies, waits for them, and re-layouts: 7.07 us -> 15.6 us
  transfers between devices with their start and end apart: 12 -> 13, of which waited for: 10 -> 10; matrix products, arithmetic and copies ran while one was open for 19% -> 20% of each run, Pallas kernels for 0% -> 0%
where the time goes in v1:
time: 430 us; the launch traced here: 425 us
  matrix products  124 us (29%)
  other arithmetic  116 us (27%)
  waiting for transfers between devices  77.8 us (18%)
  local copies, waits for them, and re-layouts  58.9 us (14%)
  starting transfers between devices  32.4 us (8%)
  blocking collectives  12.8 us (3%)
    dot_general x2, matrix products, filter_rows(): lax.dot_general(weighted, table, (((1,), (1,)), ((), ())), precision=lax....  88.2 us
    dot_general x2, other arithmetic, filter_rows(): jnp.dot(circles, table, precision=lax.Precision.HIGHEST, preferred_elemen...  76.1 us
    ppermute x2, waiting for transfers between devices, partner(): return lax.ppermute(block, axis, route)  47.5 us
    dot_general x2, matrix products, filter_rows(): jnp.dot(circles, table, precision=lax.Precision.HIGHEST, preferred_elemen...  36.2 us
    mul x8, other arithmetic, spread_flux(): term = jnp.pad(weights[position] * jump, padding)  16.7 us
    unnamed x179, local copies, waits for them, and re-layouts  15.6 us
    all_to_all x1, blocking collectives, filter_rows(): lax.all_to_all(jnp.stack(jnp.split(mixed, lax.axis_size('lon'), axis=1)),...  12.8 us
    ppermute x4, starting transfers between devices, padded_2(): before = lax.ppermute(last, axis, up)  12.1 us
  transfers between devices with their start and end apart: 13, of which 10 were waited for; matrix products, arithmetic and copies ran while one was open for 20% of the time, Pallas kernels for 0%

profile of v1, /device:TPU:9, one launch (start us, length us, event | category | flops | bytes accessed | tf_op | source)
XLA Modules:
  0.0 424.9 jit_solution(7688263944289875673)
XLA Ops:
  6.2 1.6 constant_dynamic-update-slice_fusion.31
  9.8 4.0 all-to-all-start
  13.9 38.1 %sine_select_fusion.22 = f32[1440,1440]{1,0:T(8,128)} fusion(s32[1440]{0:T(1024)S(1)} %add_select_fusion.1, pred[1440]{0:T(1024)(128)(4,1)S(1)} %get-tuple-element.271), kind=kLoop, calls=%fused_computation.3.clone.3.clone.clone.clone.clone.clone | loop fusion | flops 20736000 | bytes 8301600 | tf_op jit(solution)/shard_map/dot_general | solution.py:166
  52.2 18.1 %fusion.18 = f32[128,1440]{0,1:T(8,128)S(1)} fusion(f32[128,1440]{0,1:T(8,128)S(1)} %bitcast.233, s32[1440]{0:T(1024)S(1)} %add_select_fusion.1, f32[1440]{0:T(1024)S(1)} %select_multiply_fusion, s32[128]{0:T(128)S(1)} %get-tuple-element.54, pred[1440]{0:T(1024)(128)(4,1)S(1)} %get-tuple-element.272, f32[1440,1440]{1,0:T(8,128)} %sine_select_fusion.22), kind=kOutput, calls=%fused_computation.35 | convolution fusion | flops 3185786880 | bytes 9782432 | tf_op jit(solution)/shard_map/dot_general | solution.py:166
  70.3 44.1 %fusion.15 = f32[128,1440]{0,1:T(8,128)S(1)} fusion(f32[128,1440]{0,1:T(8,128)S(1)} %bitcast.234, f32[128,1440]{0,1:T(8,128)S(1)} %fusion.18, s32[1440]{0:T(1024)S(1)} %add_select_fusion.1, pred[1440]{0:T(1024)(128)(4,1)S(1)} %get-tuple-element.271, pred[128]{0:T(512)(128)(4,1)S(1)} %broadcast_compare_fusion.3), kind=kOutput, calls=%fused_computation.32 | convolution fusion | flops 3205969920 | bytes 2219168 | tf_op jit(solution)/shard_map/dot_general | solution.py:171
  115.4 3.8 all-to-all-start.1
  119.5 9.5 %all-to-all-done.1 = f32[4,128,360]{1,2,0:T(8,128)S(1)} async-done(((f32[4,128,360]{1,2,0:T(8,128)}), f32[4,128,360]{1,2,0:T(8,128)S(1)}, u32[]{:S(2)}, u32[]{:S(2)}) %all-to-all-start.1) | async-done | bytes 737312 | tf_op jit(solution)/shard_map/all_to_all | solution.py:180
  129.0 1.2 fusion.38
  130.2 1.6 copy.54
  131.8 4.6 %collective-permute-start = (f32[3,360,160]{1,2,0:T(8,128)S(1)}, f32[3,360,160]{1,2,0:T(8,128)}, u32[]{:S(2)}, u32[]{:S(2)}) collective-permute-start(f32[3,360,160]{1,2,0:T(8,128)S(1)} %copy.54), channel_id=1, source_target_pairs={{0,1},{1,2},{2,3},{3,4},{4,5},{5,6},{6,7},{8,9},{9,10},{10,11},{11... | collective-permute-start | bytes 2073608 | tf_op jit(solution)/shard_map/ppermute | solution.py:28
  136.4 1.2 copy.55
  137.6 1.9 collective-permute-start.1
  140.0 4.7 %collective-permute-done = f32[3,360,160]{1,2,0:T(8,128)} collective-permute-done((f32[3,360,160]{1,2,0:T(8,128)S(1)}, f32[3,360,160]{1,2,0:T(8,128)}, u32[]{:S(2)}, u32[]{:S(2)}) %collective-permute-start) | collective-permute-done | bytes 691232 | tf_op jit(solution)/shard_map/ppermute | solution.py:28
  144.8 1.5 copy.56
  146.2 4.4 %collective-permute-done.1 = f32[3,360,160]{1,2,0:T(8,128)} collective-permute-done((f32[3,360,160]{1,2,0:T(8,128)}, f32[3,360,160]{1,2,0:T(8,128)}, u32[]{:S(2)}, u32[]{:S(2)}) %collective-permute-start.1) | collective-permute-done | bytes 691232 | tf_op jit(solution)/shard_map/ppermute | solution.py:29
  150.7 2.5 copy.57
  153.2 1.5 fusion.10
  154.7 1.8 copy-done.1
  157.5 2.0 reshape.8029
  159.5 2.9 slice.1682
  162.4 2.4 copy.77
  164.8 2.9 multiply_multiply_fusion.6
  167.7 3.0 multiply_multiply_fusion.7
  173.0 1.2 collective-permute-start.2
  174.4 1.2 slice_add_fusion.11
  175.6 22.9 %collective-permute-done.2 = f32[6,360,128]{2,1,0:T(8,128)} collective-permute-done((f32[6,360,128]{2,1,0:T(8,128)}, f32[6,360,128]{2,1,0:T(8,128)}, u32[]{:S(2)}, u32[]{:S(2)}) %collective-permute-start.2) | collective-permute-done | bytes 1105952 | tf_op jit(solution)/shard_map/ppermute | solution.py:18
  198.5 1.3 fusion.231
  201.9 1.2 collective-permute-start.4
  207.5 1.4 copy.75
  208.9 1.8 multiply_multiply_fusion.23
  210.7 1.3 multiply_multiply_fusion.22
  212.4 1.3 fusion.40
  213.8 1.4 copy.63
  215.3 1.8 constant_dynamic-update-slice_fusion.63
  218.5 2.3 copy.64
  220.8 3.9 all-to-all-start.2
  224.8 38.1 %sine_select_fusion.21 = f32[1440,1440]{1,0:T(8,128)} fusion(s32[1440]{0:T(1024)S(1)} %copy-done.17, pred[1440]{0:T(1024)(128)(4,1)S(1)} %copy-done.63), kind=kLoop, calls=%fused_computation.3.clone.1.clone.clone.clone.clone.clone.1 | loop fusion | flops 20736000 | bytes 8301600 | tf_op jit(solution)/shard_map/dot_general | solution.py:166
  262.8 18.1 %fusion.17 = f32[128,1440]{0,1:T(8,128)S(1)} fusion(f32[128,1440]{0,1:T(8,128)S(1)} %bitcast.235, s32[1440]{0:T(1024)S(1)} %copy-done.17, f32[1440]{0:T(1024)S(1)} %copy-done.38, s32[128]{0:T(128)S(1)} %copy-done.66, pred[1440]{0:T(1024)(128)(4,1)S(1)} %copy-done.61, f32[1440,1440]{1,0:T(8,128)} %sine_select_fusion.21), kind=kOutput, calls=%fused_computation.34 | convolution fusion | flops 3185786880 | bytes 9782432 | tf_op jit(solution)/shard_map/dot_general | solution.py:166
  281.0 44.1 %fusion.16 = f32[128,1440]{0,1:T(8,128)S(1)} fusion(f32[128,1440]{0,1:T(8,128)S(1)} %bitcast.236, f32[128,1440]{0,1:T(8,128)S(1)} %fusion.17, s32[1440]{0:T(1024)S(1)} %copy-done.17, pred[1440]{0:T(1024)(128)(4,1)S(1)} %copy-done.63, pred[128]{0:T(512)(128)(4,1)S(1)} %copy-done.70), kind=kOutput, calls=%fused_computation.33 | convolution fusion | flops 3205969920 | bytes 2219168 | tf_op jit(solution)/shard_map/dot_general | solution.py:171
  325.2 12.8 %all_to_all.42 = f32[4,128,360]{1,2,0:T(8,128)S(1)} all-to-all(f32[4,128,360]{1,2,0:T(8,128)S(1)} %pad_maximum_fusion.9), channel_id=1, replica_groups=mesh['lon'=4,'lat'=8] {'lon'}, dimensions={0} | all-to-all | bytes 1474560 | tf_op jit(solution)/shard_map/all_to_all | solution.py:180
  338.0 1.5 fusion.37
  339.5 1.6 copy.66
  341.1 5.8 %collective-permute-start.5 = (f32[3,360,160]{1,2,0:T(8,128)S(1)}, f32[3,360,160]{1,2,0:T(8,128)}, u32[]{:S(2)}, u32[]{:S(2)}) collective-permute-start(f32[3,360,160]{1,2,0:T(8,128)S(1)} %copy.66), channel_id=1, source_target_pairs={{0,1},{1,2},{2,3},{3,4},{4,5},{5,6},{6,7},{8,9},{9,10},{10,11},{11... | collective-permute-start | bytes 2073608 | tf_op jit(solution)/shard_map/ppermute | solution.py:28
  346.9 2.5 copy.67
  349.4 1.9 collective-permute-start.6
  351.3 4.0 collective-permute-done.5
  355.3 2.5 copy.68
  357.8 4.7 %collective-permute-done.6 = f32[3,360,160]{1,2,0:T(8,128)} collective-permute-done((f32[3,360,160]{1,2,0:T(8,128)}, f32[3,360,160]{1,2,0:T(8,128)}, u32[]{:S(2)}, u32[]{:S(2)}) %collective-permute-start.6) | collective-permute-done | bytes 691232 | tf_op jit(solution)/shard_map/ppermute | solution.py:29
  362.4 2.5 copy.69
  364.9 1.8 fusion.12
  366.8 1.8 copy-done
  368.6 1.4 slice.1738
  370.0 2.0 copy.70
  372.0 1.7 broadcast_in_dim.439
  373.7 2.9 reshape.8033
  376.6 2.9 slice.1740
  379.5 2.4 copy.78
  381.9 2.9 multiply_multiply_fusion
  384.9 3.0 multiply_multiply_fusion.1
  389.4 24.6 %collective-permute-done.7 = f32[6,360,128]{2,1,0:T(8,128)S(1)} collective-permute-done((f32[6,360,128]{2,1,0:T(8,128)S(1)}, f32[6,360,128]{2,1,0:T(8,128)S(1)}, u32[]{:S(2)}, u32[]{:S(2)}) %collective-permute-start.7) | collective-permute-done | bytes 1105952 | tf_op jit(solution)/shard_map/ppermute | solution.py:18
  415.4 1.9 collective-permute-start.9
  419.8 1.4 copy.76
  421.6 1.3 multiply_multiply_fusion.16
  423.3 1.3 fusion.39
  (274 shorter events, 27.2 us)
Async XLA Ops:
  1.2 4.9 %copy-start.41 = (f32[4,360]{1,0:T(4,128)}, f32[4,360]{1,0:T(4,128)S(1)}, u32[]{:S(2)}) copy-start(f32[4,360]{1,0:T(4,128)S(1)} %get-tuple-element.255) | copy-start | bytes 17284
  1.2 4.9 %copy-start.42 = (f32[4,360]{1,0:T(4,128)}, f32[4,360]{1,0:T(4,128)S(1)}, u32[]{:S(2)}) copy-start(f32[4,360]{1,0:T(4,128)S(1)} %get-tuple-element.256) | copy-start | bytes 17284
  1.2 4.9 %copy-start.43 = (f32[4,360]{1,0:T(4,128)}, f32[4,360]{1,0:T(4,128)S(1)}, u32[]{:S(2)}) copy-start(f32[4,360]{1,0:T(4,128)S(1)} %get-tuple-element.257) | copy-start | bytes 17284
  1.2 4.9 %copy-start.44 = (f32[4,360]{1,0:T(4,128)}, f32[4,360]{1,0:T(4,128)S(1)}, u32[]{:S(2)}) copy-start(f32[4,360]{1,0:T(4,128)S(1)} %get-tuple-element.258) | copy-start | bytes 17284
  1.2 4.9 %copy-start.45 = (f32[4,360]{1,0:T(4,128)}, f32[4,360]{1,0:T(4,128)S(1)}, u32[]{:S(2)}) copy-start(f32[4,360]{1,0:T(4,128)S(1)} %get-tuple-element.259) | copy-start | bytes 17284
  1.2 4.9 %copy-start.46 = (f32[4,360]{1,0:T(4,128)}, f32[4,360]{1,0:T(4,128)S(1)}, u32[]{:S(2)}) copy-start(f32[4,360]{1,0:T(4,128)S(1)} %get-tuple-element.260) | copy-start | bytes 17284
  1.2 4.9 %copy-start.47 = (f32[4,360]{1,0:T(4,128)}, f32[4,360]{1,0:T(4,128)S(1)}, u32[]{:S(2)}) copy-start(f32[4,360]{1,0:T(4,128)S(1)} %get-tuple-element.261) | copy-start | bytes 17284
  1.2 4.9 %copy-start.48 = (f32[4,360]{1,0:T(4,128)}, f32[4,360]{1,0:T(4,128)S(1)}, u32[]{:S(2)}) copy-start(f32[4,360]{1,0:T(4,128)S(1)} %get-tuple-element.262) | copy-start | bytes 17284
  1.2 4.9 %copy-start.49 = (f32[4,360]{1,0:T(4,128)}, f32[4,360]{1,0:T(4,128)S(1)}, u32[]{:S(2)}) copy-start(f32[4,360]{1,0:T(4,128)S(1)} %get-tuple-element.263) | copy-start | bytes 17284
  1.3 4.9 %copy-start.50 = (f32[4,360]{1,0:T(4,128)}, f32[4,360]{1,0:T(4,128)S(1)}, u32[]{:S(2)}) copy-start(f32[4,360]{1,0:T(4,128)S(1)} %get-tuple-element.264) | copy-start | bytes 17284
  1.3 4.9 %copy-start.51 = (f32[4,360]{1,0:T(4,128)}, f32[4,360]{1,0:T(4,128)S(1)}, u32[]{:S(2)}) copy-start(f32[4,360]{1,0:T(4,128)S(1)} %get-tuple-element.265) | copy-start | bytes 17284
  1.7 6.1 %copy-start.20 = (f32[1,4,360]{2,1,0:T(4,128)}, f32[1,4,360]{2,1,0:T(4,128)S(1)}, u32[]{:S(2)}) copy-start(f32[1,4,360]{2,1,0:T(4,128)S(1)} %get-tuple-element.131) | copy-start | bytes 17284
  1.7 6.1 %copy-start.22 = (f32[1,4,360]{2,1,0:T(4,128)}, f32[1,4,360]{2,1,0:T(4,128)S(1)}, u32[]{:S(2)}) copy-start(f32[1,4,360]{2,1,0:T(4,128)S(1)} %get-tuple-element.133) | copy-start | bytes 17284
  1.7 6.1 %copy-start.23 = (f32[1,4,360]{2,1,0:T(4,128)}, f32[1,4,360]{2,1,0:T(4,128)S(1)}, u32[]{:S(2)}) copy-start(f32[1,4,360]{2,1,0:T(4,128)S(1)} %get-tuple-element.135) | copy-start | bytes 17284
  1.7 6.1 %copy-start.24 = (f32[1,4,360]{2,1,0:T(4,128)}, f32[1,4,360]{2,1,0:T(4,128)S(1)}, u32[]{:S(2)}) copy-start(f32[1,4,360]{2,1,0:T(4,128)S(1)} %get-tuple-element.137) | copy-start | bytes 17284
  1.8 6.1 %copy-start.25 = (f32[1,4,360]{2,1,0:T(4,128)}, f32[1,4,360]{2,1,0:T(4,128)S(1)}, u32[]{:S(2)}) copy-start(f32[1,4,360]{2,1,0:T(4,128)S(1)} %get-tuple-element.139) | copy-start | bytes 17284
  1.8 6.1 %copy-start.26 = (f32[1,4,360]{2,1,0:T(4,128)}, f32[1,4,360]{2,1,0:T(4,128)S(1)}, u32[]{:S(2)}) copy-start(f32[1,4,360]{2,1,0:T(4,128)S(1)} %get-tuple-element.141) | copy-start | bytes 17284
  1.8 6.1 %copy-start.27 = (f32[1,4,360]{2,1,0:T(4,128)}, f32[1,4,360]{2,1,0:T(4,128)S(1)}, u32[]{:S(2)}) copy-start(f32[1,4,360]{2,1,0:T(4,128)S(1)} %get-tuple-element.143) | copy-start | bytes 17284
  1.8 6.1 %copy-start.28 = (f32[1,4,360]{2,1,0:T(4,128)}, f32[1,4,360]{2,1,0:T(4,128)S(1)}, u32[]{:S(2)}) copy-start(f32[1,4,360]{2,1,0:T(4,128)S(1)} %get-tuple-element.145) | copy-start | bytes 17284
  1.8 6.1 %copy-start.29 = (f32[1,4,360]{2,1,0:T(4,128)}, f32[1,4,360]{2,1,0:T(4,128)S(1)}, u32[]{:S(2)}) copy-start(f32[1,4,360]{2,1,0:T(4,128)S(1)} %get-tuple-element.147) | copy-start | bytes 17284
  1.8 6.1 %copy-start.30 = (f32[1,4,360]{2,1,0:T(4,128)}, f32[1,4,360]{2,1,0:T(4,128)S(1)}, u32[]{:S(2)}) copy-start(f32[1,4,360]{2,1,0:T(4,128)S(1)} %get-tuple-element.149) | copy-start | bytes 17284
  1.8 6.1 %copy-start.31 = (f32[1,4,360]{2,1,0:T(4,128)}, f32[1,4,360]{2,1,0:T(4,128)S(1)}, u32[]{:S(2)}) copy-start(f32[1,4,360]{2,1,0:T(4,128)S(1)} %get-tuple-element.151) | copy-start | bytes 17284
  1.8 6.1 %copy-start.32 = (f32[1,4,360]{2,1,0:T(4,128)}, f32[1,4,360]{2,1,0:T(4,128)S(1)}, u32[]{:S(2)}) copy-start(f32[1,4,360]{2,1,0:T(4,128)S(1)} %get-tuple-element.153) | copy-start | bytes 17284
  1.8 6.1 %copy-start.33 = (f32[1,4,360]{2,1,0:T(4,128)}, f32[1,4,360]{2,1,0:T(4,128)S(1)}, u32[]{:S(2)}) copy-start(f32[1,4,360]{2,1,0:T(4,128)S(1)} %get-tuple-element.155) | copy-start | bytes 17284
  1.8 6.1 %copy-start.34 = (f32[1,4,360]{2,1,0:T(4,128)}, f32[1,4,360]{2,1,0:T(4,128)S(1)}, u32[]{:S(2)}) copy-start(f32[1,4,360]{2,1,0:T(4,128)S(1)} %get-tuple-element.157) | copy-start | bytes 17284
  1.9 6.1 %copy-start.35 = (f32[1,4,360]{2,1,0:T(4,128)}, f32[1,4,360]{2,1,0:T(4,128)S(1)}, u32[]{:S(2)}) copy-start(f32[1,4,360]{2,1,0:T(4,128)S(1)} %get-tuple-element.159) | copy-start | bytes 17284
  1.9 6.1 %copy-start.36 = (f32[1,4,360]{2,1,0:T(4,128)}, f32[1,4,360]{2,1,0:T(4,128)S(1)}, u32[]{:S(2)}) copy-start(f32[1,4,360]{2,1,0:T(4,128)S(1)} %get-tuple-element.160) | copy-start | bytes 17284
  1.9 6.1 %copy-start.14 = (f32[1,4,360]{2,1,0:T(4,128)}, f32[1,4,360]{2,1,0:T(4,128)S(1)}, u32[]{:S(2)}) copy-start(f32[1,4,360]{2,1,0:T(4,128)S(1)} %get-tuple-element.158) | copy-start | bytes 17284
  1.9 6.2 %copy-start.12 = (f32[1,4,360]{2,1,0:T(4,128)}, f32[1,4,360]{2,1,0:T(4,128)S(1)}, u32[]{:S(2)}) copy-start(f32[1,4,360]{2,1,0:T(4,128)S(1)} %get-tuple-element.156) | copy-start | bytes 17284
  1.9 6.2 %copy-start.10 = (f32[1,4,360]{2,1,0:T(4,128)}, f32[1,4,360]{2,1,0:T(4,128)S(1)}, u32[]{:S(2)}) copy-start(f32[1,4,360]{2,1,0:T(4,128)S(1)} %get-tuple-element.154) | copy-start | bytes 17284
  1.9 6.3 %copy-start.8 = (f32[1,4,360]{2,1,0:T(4,128)}, f32[1,4,360]{2,1,0:T(4,128)S(1)}, u32[]{:S(2)}) copy-start(f32[1,4,360]{2,1,0:T(4,128)S(1)} %get-tuple-element.152) | copy-start | bytes 17284
  2.9 5.1 %copy-start.55 = (f32[4,360]{1,0:T(4,128)}, f32[4,360]{1,0:T(4,128)S(1)}, u32[]{:S(2)}) copy-start(f32[4,360]{1,0:T(4,128)S(1)} %get-tuple-element.235) | copy-start | bytes 17284
  2.9 5.1 %copy-start.56 = (f32[4,360]{1,0:T(4,128)}, f32[4,360]{1,0:T(4,128)S(1)}, u32[]{:S(2)}) copy-start(f32[4,360]{1,0:T(4,128)S(1)} %get-tuple-element.236) | copy-start | bytes 17284
  2.9 5.2 %copy-start.57 = (f32[4,360]{1,0:T(4,128)}, f32[4,360]{1,0:T(4,128)S(1)}, u32[]{:S(2)}) copy-start(f32[4,360]{1,0:T(4,128)S(1)} %get-tuple-element.242) | copy-start | bytes 17284
  2.9 5.2 %copy-start.58 = (f32[4,360]{1,0:T(4,128)}, f32[4,360]{1,0:T(4,128)S(1)}, u32[]{:S(2)}) copy-start(f32[4,360]{1,0:T(4,128)S(1)} %get-tuple-element.243) | copy-start | bytes 17284
  2.9 5.2 %copy-start.59 = (f32[4,360]{1,0:T(4,128)}, f32[4,360]{1,0:T(4,128)S(1)}, u32[]{:S(2)}) copy-start(f32[4,360]{1,0:T(4,128)S(1)} %get-tuple-element.244) | copy-start | bytes 17284
  9.8 42.3 %all-to-all-start = ((f32[4,128,360]{1,2,0:T(8,128)}), f32[4,128,360]{1,2,0:T(8,128)S(1)}, u32[]{:S(2)}, u32[]{:S(2)}) async-start(f32[4,128,360]{1,2,0:T(8,128)} %copy.52), calls=%async_computation | async-start | bytes 1474560 | tf_op jit(solution)/shard_map/all_to_all | solution.py:156
  13.8 56.5 %copy-start.16 = (s32[1440]{0:T(1024)}, s32[1440]{0:T(1024)S(1)}, u32[]{:S(2)}) copy-start(s32[1440]{0:T(1024)S(1)} %add_select_fusion.1) | copy-start | bytes 17284
  13.8 38.3 %copy-start.60 = (pred[1440]{0:T(1024)(128)(4,1)}, pred[1440]{0:T(1024)(128)(4,1)S(1)}, u32[]{:S(2)}) copy-start(pred[1440]{0:T(1024)(128)(4,1)S(1)} %get-tuple-element.272) | copy-start | bytes 4324
  13.9 56.4 %copy-start.62 = (pred[1440]{0:T(1024)(128)(4,1)}, pred[1440]{0:T(1024)(128)(4,1)S(1)}, u32[]{:S(2)}) copy-start(pred[1440]{0:T(1024)(128)(4,1)S(1)} %get-tuple-element.271) | copy-start | bytes 4324
  13.9 38.1 %copy-start.67 = (s32[4]{0:T(128)S(1)}, s32[4]{0:T(128)}, u32[]{:S(2)}) copy-start(s32[4]{0:T(128)} %param.19) | copy-start | bytes 52
  13.9 38.1 %copy-start.68 = (s32[4]{0:T(128)S(1)}, s32[4]{0:T(128)}, u32[]{:S(2)}) copy-start(s32[4]{0:T(128)} %param.18) | copy-start | bytes 52
  52.0 18.3 %copy-start.37 = (f32[1440]{0:T(1024)}, f32[1440]{0:T(1024)S(1)}, u32[]{:S(2)}) copy-start(f32[1440]{0:T(1024)S(1)} %select_multiply_fusion) | copy-start | bytes 17284
  52.1 18.2 %copy-start.65 = (s32[128]{0:T(128)}, s32[128]{0:T(128)S(1)}, u32[]{:S(2)}) copy-start(s32[128]{0:T(128)S(1)} %get-tuple-element.54) | copy-start | bytes 1540
  52.1 18.2 %copy-start.69 = (pred[128]{0:T(512)(128)(4,1)}, pred[128]{0:T(512)(128)(4,1)S(1)}, u32[]{:S(2)}) copy-start(pred[128]{0:T(512)(128)(4,1)S(1)} %broadcast_compare_fusion.3) | copy-start | bytes 388
  115.4 13.6 %all-to-all-start.1 = ((f32[4,128,360]{1,2,0:T(8,128)}), f32[4,128,360]{1,2,0:T(8,128)S(1)}, u32[]{:S(2)}, u32[]{:S(2)}) async-start(f32[4,128,360]{1,2,0:T(8,128)} %pad_maximum_fusion.8), calls=%async_computation.1 | async-start | bytes 1474560 | tf_op jit(solution)/shard_map/all_to_all | solution.py:180
  129.0 24.2 %copy-start.2 = (f32[4,128,360]{1,2,0:T(8,128)}, f32[4,128,360]{1,2,0:T(8,128)S(1)}, u32[]{:S(2)}) copy-start(f32[4,128,360]{1,2,0:T(8,128)S(1)} %all-to-all-done.1) | copy-start | bytes 2211844
  131.8 13.0 %collective-permute-start = (f32[3,360,160]{1,2,0:T(8,128)S(1)}, f32[3,360,160]{1,2,0:T(8,128)}, u32[]{:S(2)}, u32[]{:S(2)}) collective-permute-start(f32[3,360,160]{1,2,0:T(8,128)S(1)} %copy.54), channel_id=1, source_target_pairs={{0,1},{1,2},{2,3},{3,4},{4,5},{5,6},{6,7},{8,9},{9,10},{10,11},{11... | collective-permute-start | bytes 2073608 | tf_op jit(solution)/shard_map/ppermute | solution.py:28
  137.6 13.1 %collective-permute-start.1 = (f32[3,360,160]{1,2,0:T(8,128)}, f32[3,360,160]{1,2,0:T(8,128)}, u32[]{:S(2)}, u32[]{:S(2)}) collective-permute-start(f32[3,360,160]{1,2,0:T(8,128)} %copy.55), channel_id=1, source_target_pairs={{1,0},{2,1},{3,2},{4,3},{5,4},{6,5},{7,6},{9,8},{10,9},{11,10},{12... | collective-permute-start | bytes 2073608 | tf_op jit(solution)/shard_map/ppermute | solution.py:29
  173.0 25.5 %collective-permute-start.2 = (f32[6,360,128]{2,1,0:T(8,128)}, f32[6,360,128]{2,1,0:T(8,128)}, u32[]{:S(2)}, u32[]{:S(2)}) collective-permute-start(f32[6,360,128]{2,1,0:T(8,128)} %pad_maximum_fusion.6), channel_id=1, source_target_pairs={{0,16},{16,0},{8,24},{24,8},{1,17},{17,1},{9,25},{25,9},{2,18},{18... | collective-permute-start | bytes 3317768 | tf_op jit(solution)/shard_map/ppermute | solution.py:18
  200.7 3.5 collective-permute-start.3
  201.9 3.1 collective-permute-start.4
  217.5 7.2 %copy-start.17 = (s32[1440]{0:T(1024)S(1)}, s32[1440]{0:T(1024)}, u32[]{:S(2)}) copy-start(s32[1440]{0:T(1024)} %copy-done.16) | copy-start | bytes 17284
  217.5 7.2 %copy-start.63 = (pred[1440]{0:T(1024)(128)(4,1)S(1)}, pred[1440]{0:T(1024)(128)(4,1)}, u32[]{:S(2)}) copy-start(pred[1440]{0:T(1024)(128)(4,1)} %copy-done.62) | copy-start | bytes 4324
  220.8 42.0 %all-to-all-start.2 = ((f32[4,128,360]{1,2,0:T(8,128)}), f32[4,128,360]{1,2,0:T(8,128)S(1)}, u32[]{:S(2)}, u32[]{:S(2)}) async-start(f32[4,128,360]{1,2,0:T(8,128)} %copy.64), calls=%async_computation.2 | async-start | bytes 1474560 | tf_op jit(solution)/shard_map/all_to_all | solution.py:156
  224.7 38.1 %copy-start.38 = (f32[1440]{0:T(1024)S(1)}, f32[1440]{0:T(1024)}, u32[]{:S(2)}) copy-start(f32[1440]{0:T(1024)} %copy-done.37) | copy-start | bytes 17284
  224.7 38.1 %copy-start.61 = (pred[1440]{0:T(1024)(128)(4,1)S(1)}, pred[1440]{0:T(1024)(128)(4,1)}, u32[]{:S(2)}) copy-start(pred[1440]{0:T(1024)(128)(4,1)} %copy-done.60) | copy-start | bytes 4324
  224.7 38.1 %copy-start.66 = (s32[128]{0:T(128)S(1)}, s32[128]{0:T(128)}, u32[]{:S(2)}) copy-start(s32[128]{0:T(128)} %copy-done.65) | copy-start | bytes 1540
  262.8 18.1 %copy-start.70 = (pred[128]{0:T(512)(128)(4,1)S(1)}, pred[128]{0:T(512)(128)(4,1)}, u32[]{:S(2)}) copy-start(pred[128]{0:T(512)(128)(4,1)} %copy-done.69) | copy-start | bytes 388
  341.1 14.2 %collective-permute-start.5 = (f32[3,360,160]{1,2,0:T(8,128)S(1)}, f32[3,360,160]{1,2,0:T(8,128)}, u32[]{:S(2)}, u32[]{:S(2)}) collective-permute-start(f32[3,360,160]{1,2,0:T(8,128)S(1)} %copy.66), channel_id=1, source_target_pairs={{0,1},{1,2},{2,3},{3,4},{4,5},{5,6},{6,7},{8,9},{9,10},{10,11},{11... | collective-permute-start | bytes 2073608 | tf_op jit(solution)/shard_map/ppermute | solution.py:28
  349.4 13.1 %collective-permute-start.6 = (f32[3,360,160]{1,2,0:T(8,128)}, f32[3,360,160]{1,2,0:T(8,128)}, u32[]{:S(2)}, u32[]{:S(2)}) collective-permute-start(f32[3,360,160]{1,2,0:T(8,128)} %copy.67), channel_id=1, source_target_pairs={{1,0},{2,1},{3,2},{4,3},{5,4},{6,5},{7,6},{9,8},{10,9},{11,10},{12... | collective-permute-start | bytes 2073608 | tf_op jit(solution)/shard_map/ppermute | solution.py:29
  388.7 25.3 %collective-permute-start.7 = (f32[6,360,128]{2,1,0:T(8,128)S(1)}, f32[6,360,128]{2,1,0:T(8,128)S(1)}, u32[]{:S(2)}, u32[]{:S(2)}) collective-permute-start(f32[6,360,128]{2,1,0:T(8,128)S(1)} %pad_maximum_fusion.7), channel_id=1, source_target_pairs={{0,16},{16,0},{8,24},{24,8},{1,17},{17,1},{9,25},{25,9},{2,18},{18... | collective-permute-start | bytes 3317768 | tf_op jit(solution)/shard_map/ppermute | solution.py:18
  414.8 3.5 collective-permute-start.8
  415.4 3.0 collective-permute-start.9
  (20 other events, 52.2 us)
